TPU v7x, 256 devices: a whole 4x4x8 slice. The times are simulated.
256 devices in a mesh: seq: 64 (over z, x, y_lo), head: 4 (over y_hi, core).
Axes of the slice: x: 4, y: 4 (y_hi: 2, y_lo: 2; y = y_hi * 2 + y_lo), z: 8, core: 2. Of those that a mesh axis runs over, the one named last changes fastest.
Arguments:
- queries: bfloat16 [16384, 512], P('seq', 'head'), may hold values from -32 to 32
- keys: bfloat16 [16384, 512], P('seq', 'head'), may hold values from -32 to 32
- values: bfloat16 [16384, 512], P('seq', 'head'), may hold values from -6 to 6
- d_out: bfloat16 [16384, 512], P('seq', 'head'), may hold values from -6 to 6
Outputs:
- d_queries: bfloat16 [16384, 512], P('seq')
- d_keys: bfloat16 [16384, 512], P('seq')
- d_values: bfloat16 [16384, 512], P('seq')
All inputs are finite; a program needn't handle non-finite values.
Results may differ from a plain program's by a relative error of at most 0.008.
Values may be sent and summed in bfloat16 or wider, within the bound.
A program may use at most 128 MiB of HBM per device.

v0:
```python
import math

import jax
import jax.numpy as jnp
from jax import lax
from jax.sharding import PartitionSpec as P

HEAD_DIM = 128


def local(queries, keys, values, d_out):
    width = queries.shape[1]
    head_dim = HEAD_DIM
    scale = 1.0 / math.sqrt(head_dim)
    rows = queries.shape[0]
    local_heads = width // head_dim
    shape_three = (rows, local_heads, head_dim)
    query_three = queries.reshape(shape_three)
    cot_three = d_out.reshape(shape_three)
    key_all, value_all = (
        lax.all_gather(keys, "seq", axis=0, tiled=True),
        lax.all_gather(values, "seq", axis=0, tiled=True),
    )
    total = key_all.shape[0]
    block = math.gcd(total, 1024)
    count_blocks = total // block
    key_blocks = key_all.reshape(count_blocks, block, local_heads, head_dim)
    value_blocks = value_all.reshape(count_blocks, block, local_heads, head_dim)

    def stat_step(index, carry):
        top, mass, weighted = carry
        scores = (
            jnp.einsum(
                "shd,khd->hsk", query_three, key_blocks[index], preferred_element_type=jnp.float32
            )
            * scale
        )
        d_probs = jnp.einsum(
            "shd,khd->hsk", cot_three, value_blocks[index], preferred_element_type=jnp.float32
        )
        new_top = jnp.maximum(top, jnp.max(scores, axis=-1))
        fade = jnp.exp(top - new_top)
        expo = jnp.exp(scores - new_top[..., None])
        return (
            new_top,
            mass * fade + jnp.sum(expo, axis=-1),
            weighted * fade + jnp.sum(expo * d_probs, axis=-1),
        )

    start_top = jnp.full((local_heads, rows), -jnp.inf, jnp.float32)
    zeros_stat = jnp.zeros((local_heads, rows), jnp.float32)
    top, mass, weighted = lax.fori_loop(
        0, count_blocks, stat_step, (start_top, zeros_stat, zeros_stat)
    )
    lse = top + jnp.log(mass)
    delta = weighted / mass

    def probs_of(key_block, value_block):
        scores = (
            jnp.einsum("shd,khd->hsk", query_three, key_block, preferred_element_type=jnp.float32)
            * scale
        )
        d_probs = jnp.einsum(
            "shd,khd->hsk", cot_three, value_block, preferred_element_type=jnp.float32
        )
        probs = jnp.exp(scores - lse[..., None])
        return (probs, probs * (d_probs - delta[..., None]))

    empty = jnp.zeros(shape_three, jnp.float32)

    def grad_step(index, carry):
        query_grad, partial_value = carry
        key_block = key_blocks[index]
        probs, d_scores = probs_of(key_block, value_blocks[index])
        d_low = d_scores.astype(jnp.bfloat16)
        query_grad = query_grad + jnp.einsum(
            "hsk,khd->shd", d_low, key_block, preferred_element_type=jnp.float32
        )
        key_term = (
            jnp.einsum("hsk,shd->khd", d_low, query_three, preferred_element_type=jnp.float32)
            * scale
        )
        value_term = jnp.einsum(
            "hsk,shd->khd",
            probs.astype(jnp.bfloat16),
            cot_three,
            preferred_element_type=jnp.float32,
        )
        piece = jnp.concatenate(
            (key_term.reshape(block, width), value_term.reshape(block, width)), axis=1
        )
        partial_value = lax.dynamic_update_slice_in_dim(partial_value, piece, index * block, 0)
        return (query_grad, partial_value)

    start_partial = jnp.zeros((total, 2 * width), jnp.float32)
    query_grad, partial_value = lax.fori_loop(0, count_blocks, grad_step, (empty, start_partial))
    summed = lax.psum_scatter(partial_value, "seq", scatter_dimension=0, tiled=True)
    d_key = summed[:, :width].astype(jnp.bfloat16)
    d_value = summed[:, width:].astype(jnp.bfloat16)
    d_query = (query_grad * scale).astype(jnp.bfloat16).reshape(rows, width)
    all_query, all_key, all_value = (
        lax.all_gather(d_query, "head", axis=1, tiled=True),
        lax.all_gather(d_key, "head", axis=1, tiled=True),
        lax.all_gather(d_value, "head", axis=1, tiled=True),
    )
    return (all_query, all_key, all_value)


def solution(mesh):
    in_specs = (P("seq", "head"), P("seq", "head"), P("seq", "head"), P("seq", "head"))
    out_specs = (P("seq", None), P("seq", None), P("seq", None))
    return jax.shard_map(local, mesh=mesh, in_specs=in_specs, out_specs=out_specs, check_vma=False)
```

profile of v0, /device:TPU:1, one launch (start us, length us, event | category | flops | bytes accessed | tf_op | source)
XLA Modules:
  0.0 1164.4 jit_solution(4494769265979152076)
XLA Ops:
  8.7 265.8 %all-gather.4.cloned.1.call-done = bf16[16384,128]{1,0:T(8,128)(2,1)} async-done(((bf16[256,128]{1,0:T(8,128)(2,1)}), bf16[16384,128]{1,0:T(8,128)(2,1)}) %all-gather.4.cloned.1.call-update) | async-done | bytes 4194320 | tf_op jit(solution)/shard_map/all_gather | solution.py:21
  274.5 303.4 %all-gather.6.cloned.1.call-done = bf16[16384,128]{1,0:T(8,128)(2,1)} async-done(((bf16[256,128]{1,0:T(8,128)(2,1)}), bf16[16384,128]{1,0:T(8,128)(2,1)}) %all-gather.6.cloned.1.call-update) | async-done | bytes 4194320 | tf_op jit(solution)/shard_map/all_gather | solution.py:22
  577.9 46.9 %while.34 = (s32[]{:T(128)}, f32[1,256]{1,0:T(1,128)S(1)}, f32[1,256]{1,0:T(1,128)S(1)}, f32[1,256]{1,0:T(1,128)S(1)}, bf16[16,1024,1,128]{3,1,2,0:T(8,128)(2,1)...) while((s32[]{:T(128)}, f32[1,256]{1,0:T(1,128)S(1)}, ...), condition=%wide.region_4.0_spmd.clone, body=%wide.region_0.0_spmd.clone.sunk | while | flops 136054528 | bytes 3819648 | solution.py:52
  579.2 1.3 fusion.65
  582.1 1.3 fusion.65
  585.0 1.3 fusion.65
  588.0 1.3 fusion.65
  590.9 1.3 fusion.65
  593.8 1.3 fusion.65
  596.7 1.3 fusion.65
  599.7 1.3 fusion.65
  602.6 1.3 fusion.65
  605.5 1.3 fusion.65
  611.4 1.3 fusion.65
  614.3 1.3 fusion.65
  617.3 1.3 fusion.65
  620.2 1.3 fusion.65
  623.1 1.3 fusion.65
  624.8 6.0 broadcast_in_dim.22.clone
  630.8 94.8 %while.35 = (s32[]{:T(128)}, f32[256,1,128]{0,2,1:T(8,128)S(1)}, f32[16384,256]{1,0:T(8,128)}, bf16[16,1024,1,128]{3,1,2,0:T(8,128)(2,1)}, bf16[256,1,128]{2,0,1...) while((s32[]{:T(128)}, f32[256,1,128]{0,2,1:T(8,128)S(1)}, ...), condition=%wide.region_6.0_spmd.clone, body=%wide.region_5.0_spmd.clone.sunk | while | flops 337575936 | bytes 13371597 | solution.py:96
  725.7 51.3 %all-gather = bf16[256,1,512]{2,0,1:T(8,128)(2,1)S(1)} all-gather(bf16[256,1,128]{2,0,1:T(8,128)(2,1)S(1)} %multiply_convert_fusion), channel_id=2, replica_groups=mesh['seq'=64,'head'=4] {'head'}, dimensions={2}, use_global_device_ids=true | all-gather | bytes 327680 | tf_op jit(solution)/shard_map/all_gather | solution.py:102
  777.1 359.8 %reduce-scatter.2.cloned.1.call-done = f32[256,256]{1,0:T(8,128)} async-done(((f32[16384,256]{1,0:T(8,128)}), f32[256,256]{1,0:T(8,128)}) %reduce-scatter.2.cloned.1.call-update) | async-done | bytes 262160 | tf_op jit(solution)/shard_map/reduce_scatter | solution.py:97
  1137.8 10.5 all_gather.19
  1148.3 7.4 all_gather.18
  (231 shorter events, 124.8 us)
Async XLA Ops:
  7.2 267.3 %all-gather.4.cloned.1.call-start = ((), (), s32[]{:S(2)}) async-start(), calls=%async_computation.1 | async-start | bytes 4259840 | tf_op jit(solution)/shard_map/all_gather | solution.py:21
  7.9 570.0 %all-gather.6.cloned.1.call-start = ((), (), s32[]{:S(2)}) async-start(), calls=%async_computation.2 | async-start | bytes 4259840 | tf_op jit(solution)/shard_map/all_gather | solution.py:22
  8.6 1128.2 %reduce-scatter.2.cloned.1.call-start = ((), (), s32[]{:S(2)}) async-start(), calls=%async_computation.3 | async-start | bytes 17039360 | tf_op jit(solution)/shard_map/reduce_scatter | solution.py:97
  624.7 6.0 copy-start
  624.8 6.0 copy-start.1
Sparse Core Ops, SparseCore 0:
  9.8 264.6 all-gather.3
  276.3 301.5 all-gather.5
  725.7 411.0 reduce-scatter.1
where the time goes:
time: 1170 us; the launch traced here: 1160 us
  waiting for transfers between devices  930 us (79%)
  matrix products  112 us (10%)
  blocking collectives  69.3 us (6%)
  local copies, waits for them, and re-layouts  30.7 us (3%)
  between operations  13.8 us (1%)
    reduce_scatter x1, waiting for transfers between devices, local(): lax.psum_scatter(partial_value, 'seq', scatter_dimension=0, tiled=True)  360 us
    all_gather x1, waiting for transfers between devices, local(): lax.all_gather(values, 'seq', axis=0, tiled=True)  303 us
    all_gather x1, waiting for transfers between devices, local(): lax.all_gather(keys, 'seq', axis=0, tiled=True)  266 us
    all_gather x1, blocking collectives, local(): lax.all_gather(d_query, 'head', axis=1, tiled=True)  51.3 us
  transfers between devices with their start and end apart: 3, of which 3 were waited for; matrix products, arithmetic and copies ran while one was open for 0% of the time, Pallas kernels for 0%

commit v1 on v0

v1 whole, which is shorter than its diff:
```python
import math

import jax
import jax.numpy as jnp
from jax import lax
from jax.experimental import pallas as pl
from jax.experimental.pallas import tpu as pltpu
from jax.sharding import PartitionSpec as P

HEAD_DIM = 128
NZ, NX, NY = 8, 4, 2
NXY = NX * NY
NCORE = 2
SCALE = 1.0 / math.sqrt(HEAD_DIM)
LOG2E_SCALE = math.log2(math.e) * SCALE
MESH = pl.DeviceIdType.MESH
F32 = jnp.float32
BF16 = jnp.bfloat16
NT = (((1,), (1,)), ((), ()))
NN = (((1,), (0,)), ((), ()))


def dot(a, b, dims):
    return lax.dot_general(a, b, dims, preferred_element_type=F32)


Z_AT = [0, 1, -1, 2, -2, 3, -3, 4]
XY_AT = [(0, 0), (0, 1), (1, 0), (-1, 0), (1, 1), (-1, 1), (2, 0), (2, 1)]


def kernel(
    q_in,
    k_in,
    v_in,
    do_in,
    oq,
    ok,
    ov,
    qd,
    kv,
    scores,
    dprobs,
    top,
    mass,
    weighted,
    st_own,
    st_all,
    lse,
    delta,
    dqt,
    pkv,
    send_anti,
    recv_anti,
    send_one,
    recv_one,
    send_y,
    recv_y,
    zsend,
    zrecv4,
    zrecv,
    fin,
    local_sem,
    send_sem,
    recv_sem,
):
    rows = q_in.shape[0]
    total_q = NZ * rows
    total_k = NXY * rows
    seq = lax.axis_index("seq")
    head = lax.axis_index("head")
    z = seq // NXY
    x = (seq // NY) % NX
    y = seq % NY

    def at(dz=0, dx=0, dy=0):
        zz = (z + dz + NZ) % NZ
        xx = (x + dx + NX) % NX
        yy = (y + dy) % NY
        return (zz * NXY + xx * NY + yy, head)

    def head_at(dh):
        return (seq, (head + dh) % (2 * NCORE))

    counter = [0]
    sent = []

    def remote(src, dst, device):
        i = counter[0]
        counter[0] += 1
        c = pltpu.make_async_remote_copy(
            src_ref=src,
            dst_ref=dst,
            send_sem=send_sem.at[i],
            recv_sem=recv_sem.at[i],
            device_id=device,
            device_id_type=MESH,
        )
        sent.append(c)
        return c

    own = [
        pltpu.make_async_copy(src, dst, local_sem.at[i])
        for i, (src, dst) in enumerate(
            [
                (q_in, qd.at[0, 0]),
                (do_in, qd.at[1, 0]),
                (k_in, kv.at[0, 0]),
                (v_in, kv.at[1, 0]),
            ]
        )
    ]
    for c in own:
        c.start()

    barrier = pltpu.get_barrier_semaphore()
    peers = [at(dz=d) for d in range(1, NZ)]
    peers += [at(dx=1), at(dx=-1), at(dy=1)]
    peers += [head_at(d) for d in range(1, 2 * NCORE)]
    for p in peers:
        pl.semaphore_signal(barrier, inc=1, device_id=p, device_id_type=MESH)
    for c in own:
        c.wait()
    pl.semaphore_wait(barrier, len(peers))

    zc = {}
    for part in range(2):
        zc[2, part] = remote(qd.at[part, 0], qd.at[part, 2], at(dz=1))
        zc[1, part] = remote(qd.at[part, 0], qd.at[part, 1], at(dz=-1))
    kc = {}
    for part in range(2):
        kc[3, part] = remote(kv.at[part, 0], kv.at[part, 3], at(dx=1))
        kc[2, part] = remote(kv.at[part, 0], kv.at[part, 2], at(dx=-1))
        kc[1, part] = remote(kv.at[part, 0], kv.at[part, 1], at(dy=1))
    for part in range(2):
        for c in (zc[2, part], zc[1, part], kc[3, part], kc[2, part], kc[1, part]):
            c.start()

    def z_forward(a, part):
        zc[a, part].wait_recv()
        b = a + 2
        if b < 7:
            zc[b, part] = remote(
                qd.at[part, a], qd.at[part, b], at(dz=-1 if a % 2 else 1)
            )
            zc[b, part].start()
        elif (a == 6) == (part == 0):
            zc[7, part] = remote(
                qd.at[part, a], qd.at[part, 7], at(dz=-1 if a % 2 else 1)
            )
            zc[7, part].start()

    for part in range(2):
        z_forward(2, part)
        z_forward(1, part)
        kc[1, part].wait_recv()
        kc[5, part] = remote(kv.at[part, 1], kv.at[part, 5], at(dx=1))
        kc[4, part] = remote(kv.at[part, 1], kv.at[part, 4], at(dx=-1))
        kc[5, part].start()
        kc[4, part].start()
        kc[3, part].wait_recv()
        kc[2, part].wait_recv()
        if part == 0:
            kc[6, 0] = remote(kv.at[0, 3], kv.at[0, 6], at(dx=1))
            kc[6, 0].start()
        else:
            kc[6, 1] = remote(kv.at[1, 2], kv.at[1, 6], at(dx=-1))
            kc[6, 1].start()
    for part in range(2):
        z_forward(4, part)
        z_forward(3, part)
    for part in range(2):
        kc[6, part].wait_recv()
        kc[7, part] = remote(kv.at[part, 6], kv.at[part, 7], at(dy=1))
        kc[7, part].start()
    for part in range(2):
        z_forward(6, part)
        z_forward(5, part)
    for part in range(2):
        kc[5, part].wait_recv()
        kc[4, part].wait_recv()
    for part in range(2):
        kc[7, part].wait_recv()
    for part in range(2):
        zc[7, part].wait_recv()

    qb = 2 * rows

    @pl.loop(0, NZ // 2)
    def _(i):
        qs = pl.ds(pl.multiple_of(i * qb, qb), qb)
        two = pl.ds(pl.multiple_of(i * 2, 2), 2)
        qq = qd[0, two].reshape(qb, HEAD_DIM)
        dd = qd[1, two].reshape(qb, HEAD_DIM)
        s = dot(kv[0].reshape(total_k, HEAD_DIM), qq, NT)
        scores[:, qs] = s
        m = jnp.max(s, axis=0, keepdims=True) * LOG2E_SCALE
        e = jnp.exp2(s * LOG2E_SCALE - m)
        dp = dot(kv[1].reshape(total_k, HEAD_DIM), dd, NT)
        dprobs[:, qs] = dp
        l = jnp.sum(e, axis=0, keepdims=True)
        w = jnp.sum(e * dp, axis=0, keepdims=True)
        top[:, qs] = m + jnp.log2(l)
        weighted[:, qs] = w / l

    for slot, dz in enumerate(Z_AT):
        o = (z + dz + NZ) % NZ
        st_own[0, pl.ds(o, 1), :] = top[:, pl.ds(slot * rows, rows)]
        st_own[1, pl.ds(o, 1), :] = weighted[:, pl.ds(slot * rows, rows)]
    sc = []
    for d in range(1, NZ):
        c = remote(st_own, st_all.at[d], at(dz=d))
        c.start()
        sc.append(c)
    st_all[0] = st_own[...]
    for c in sc:
        c.wait_recv()
    big = st_all[0, 0]
    for d in range(1, NZ):
        big = jnp.maximum(big, st_all[d, 0])
    mass_all = jnp.zeros_like(big)
    weighted_all = jnp.zeros_like(big)
    for d in range(NZ):
        f = jnp.exp2(st_all[d, 0] - big)
        mass_all += f
        weighted_all += f * st_all[d, 1]
    for c in sc:
        c.wait_send()
    st_own[0] = big + jnp.log2(mass_all)
    st_own[1] = weighted_all / mass_all
    for slot, dz in enumerate(Z_AT):
        o = (z + dz + NZ) % NZ
        lse[:, pl.ds(slot * rows, rows)] = st_own[0, pl.ds(o, 1), :]
        delta[:, pl.ds(slot * rows, rows)] = st_own[1, pl.ds(o, 1), :]

    dqt[...] = jnp.zeros(dqt.shape, F32)
    anti = {}
    for dy in range(2):
        anti[0, dy] = remote(send_anti.at[0, dy], recv_anti.at[0, dy], at(dx=1))
        anti[1, dy] = remote(send_anti.at[1, dy], recv_anti.at[1, dy], at(dx=-1))
    one = {}
    for dy in range(2):
        one[0, dy] = remote(send_one.at[0, dy], recv_one.at[0, dy], at(dx=1))
        one[1, dy] = remote(send_one.at[1, dy], recv_one.at[1, dy], at(dx=-1))
    ycopy = remote(send_y, recv_y, at(dy=1))

    @pl.loop(0, NXY)
    def _(it):
        slot = NXY - 1 - it
        ks = pl.ds(pl.multiple_of(slot * rows, rows), rows)
        kk = kv[0, slot]
        p = jnp.exp2(scores[ks, :] * LOG2E_SCALE - lse[...])
        ds = (p * (dprobs[ks, :] - delta[...])).astype(BF16)
        pkv[1] = dot(p.astype(BF16), qd[1].reshape(total_q, HEAD_DIM), NN)
        pkv[0] = dot(ds, qd[0].reshape(total_q, HEAD_DIM), NN) * SCALE
        dqt[...] += dot(kk.T, ds, NN)

        for dy in range(2):

            @pl.when(slot == 6 + dy)
            def _():
                for part in range(2):
                    send_anti[part, dy] = pkv[part].astype(BF16)
                    anti[part, dy].start()

            for side in range(2):

                @pl.when(slot == 2 + 2 * dy + side)
                def _():
                    anti[side, dy].wait_recv()
                    send_one[side, dy, side] = (
                        pkv[side] + recv_anti[side, dy].astype(F32)
                    ).astype(BF16)
                    send_one[side, dy, 1 - side] = pkv[1 - side].astype(BF16)
                    one[side, dy].start()

        @pl.when(slot == 1)
        def _():
            one[0, 1].wait_recv()
            one[1, 1].wait_recv()
            for part in range(2):
                send_y[part] = (
                    pkv[part]
                    + recv_one[0, 1, part].astype(F32)
                    + recv_one[1, 1, part].astype(F32)
                ).astype(BF16)
            ycopy.start()

    half = rows // 2

    def mine(slot):
        return dqt[:, pl.ds(slot * rows, rows)].T * SCALE

    t = mine(7)
    zsend[0, 0] = t.astype(BF16)
    far = [
        remote(zsend.at[0, 0, pl.ds(0, half)], zrecv4.at[0], at(dz=1)),
        remote(zsend.at[0, 0, pl.ds(half, half)], zrecv4.at[1], at(dz=-1)),
    ]
    for c in far:
        c.start()
    before = None
    for hop in range(3):
        now = []
        for side in range(2):
            own_part = mine(5 - 2 * hop + side)
            if hop == 0:
                far[side].wait_recv()
                lo = own_part[:half]
                hi = own_part[half:]
                if side == 0:
                    lo = lo + zrecv4[0].astype(F32)
                else:
                    hi = hi + zrecv4[1].astype(F32)
                zsend[side, 1, pl.ds(0, half)] = lo.astype(BF16)
                zsend[side, 1, pl.ds(half, half)] = hi.astype(BF16)
            else:
                before[side].wait_recv()
                zsend[side, 1 + hop] = (
                    own_part + zrecv[side, hop - 1].astype(F32)
                ).astype(BF16)
            c = remote(
                zsend.at[side, 1 + hop], zrecv.at[side, hop], at(dz=1 - 2 * side)
            )
            c.start()
            now.append(c)
        before = now

    def finish(index, out):
        cols = pl.ds(pl.multiple_of(head * HEAD_DIM, HEAD_DIM), HEAD_DIM)
        cs = [
            remote(fin.at[index], out.at[:, cols], head_at(d))
            for d in range(1, 2 * NCORE)
        ]
        c0 = pltpu.make_async_copy(fin.at[index], out.at[:, cols], local_sem.at[index])
        for c in cs:
            c.start()
        c0.start()
        return c0, cs

    one[0, 0].wait_recv()
    one[1, 0].wait_recv()
    ycopy.wait_recv()
    ends = []
    for part, out in ((0, ok), (1, ov)):
        fin[part] = (
            pkv[part]
            + recv_one[0, 0, part].astype(F32)
            + recv_one[1, 0, part].astype(F32)
            + recv_y[part].astype(F32)
        ).astype(BF16)
        ends.append(finish(part, out))
    own_part = mine(0)
    for side in range(2):
        before[side].wait_recv()
    fin[2] = (
        own_part + zrecv[0, 2].astype(F32) + zrecv[1, 2].astype(F32)
    ).astype(BF16)
    ends.append(finish(2, oq))
    for c0, cs in ends:
        c0.wait()
        for c in cs:
            c.wait_recv()
    for c in sent:
        if not any(c is s for s in sc):
            c.wait_send()


def local(queries, keys, values, d_out):
    rows, width = queries.shape
    total = NZ * rows
    any_spec = pl.BlockSpec(memory_space=pl.ANY)
    out = jax.ShapeDtypeStruct((rows, 2 * NCORE * width), BF16)
    vm = pltpu.VMEM
    return pl.pallas_call(
        kernel,
        out_shape=[out, out, out],
        in_specs=[any_spec] * 4,
        out_specs=[any_spec] * 3,
        scratch_shapes=[
            vm((2, NZ, rows, width), BF16),
            vm((2, NXY, rows, width), BF16),
            vm((total, total), F32),
            vm((total, total), F32),
            vm((1, total), F32),
            vm((1, total), F32),
            vm((1, total), F32),
            vm((2, NZ, rows), F32),
            vm((NZ, 2, NZ, rows), F32),
            vm((1, total), F32),
            vm((1, total), F32),
            vm((width, total), F32),
            vm((2, rows, width), F32),
            vm((2, 2, rows, width), BF16),
            vm((2, 2, rows, width), BF16),
            vm((2, 2, 2, rows, width), BF16),
            vm((2, 2, 2, rows, width), BF16),
            vm((2, rows, width), BF16),
            vm((2, rows, width), BF16),
            vm((2, 4, rows, width), BF16),
            vm((2, rows // 2, width), BF16),
            vm((2, 3, rows, width), BF16),
            vm((3, rows, width), BF16),
            pltpu.SemaphoreType.DMA((4,)),
            pltpu.SemaphoreType.DMA((72,)),
            pltpu.SemaphoreType.DMA((72,)),
        ],
        compiler_params=pltpu.CompilerParams(
            collective_id=0, has_side_effects=True, vmem_limit_bytes=58 * 2**20
        ),
        name="attention_backward",
    )(queries, keys, values, d_out)


def solution(mesh):
    in_specs = (P("seq", "head"), P("seq", "head"), P("seq", "head"), P("seq", "head"))
    out_specs = (P("seq", None), P("seq", None), P("seq", None))
    return jax.shard_map(local, mesh=mesh, in_specs=in_specs, out_specs=out_specs, check_vma=False)
```

time: 1170 us -> 76.2 us (0.07)
  waiting for transfers between devices: 930 us -> 0 us
  matrix products: 112 us -> 0 us
  Pallas kernels: 0 us -> 71.9 us
  blocking collectives: 69.3 us -> 0 us
  local copies, waits for them, and re-layouts: 30.7 us -> 3.46 us
  between operations: 13.8 us -> 0.65 us
    all_gather x2 -> x0, waiting for transfers between devices: 569 us -> none  [the longest x1 303 us: local(): lax.all_gather(values, 'seq', axis=0, tiled=True)]
    reduce_scatter x1 -> x0, waiting for transfers between devices: 360 us -> none  [local(): lax.psum_scatter(partial_value, 'seq', scatter_dimension=0, tiled=True)]
    dot_general x112 -> x0, matrix products: 112 us -> none  [the longest x16 21.5 us: stat_step(): jnp.einsum('shd,khd->hsk', cot_three, value_blocks[index], preferred_elem...]
    pallas_call x0 -> x1, Pallas kernels: none -> 71.9 us  [local(): pl.pallas_call(kernel, out_shape=[out, out, out], in_specs=[any_spec] * 4...]
    all_gather x3 -> x0, blocking collectives: 69.3 us -> none  [the longest x1 51.3 us: local(): lax.all_gather(d_query, 'head', axis=1, tiled=True)]
    dynamic_update_slice x32 -> x0, local copies, waits for them, and re-layouts: 22.5 us -> none  [grad_step(): lax.dynamic_update_slice_in_dim(partial_value, piece, index * block, 0)]
  transfers between devices with their start and end apart: 3 -> 0, of which waited for: 3 -> 0; matrix products, arithmetic and copies ran while one was open for 0% -> 0% of each run, Pallas kernels for 0% -> 0%
where the time goes in v1:
time: 76.2 us; the launch traced here: 76 us
  Pallas kernels  71.9 us (94%)
  local copies, waits for them, and re-layouts  3.46 us (5%)
    pallas_call x1, Pallas kernels, local(): pl.pallas_call(kernel, out_shape=[out, out, out], in_specs=[any_spec] * 4...  71.9 us
    unnamed x7, local copies, waits for them, and re-layouts  3.46 us

profile of v1, /device:TPU:1, one launch (start us, length us, event | category | flops | bytes accessed | tf_op | source)
XLA Modules:
  0.0 76.0 jit_solution(12627510713861319043)
XLA Ops:
  0.6 71.9 %attention_backward.1 = (bf16[256,512]{1,0:T(8,128)(2,1)}, bf16[256,512]{1,0:T(8,128)(2,1)}, bf16[256,512]{1,0:T(8,128)(2,1)}) custom-call(bf16[256,128]{1,0:T(8,128)(2,1)} %q_in.1, bf16[256,128]{1,0:T(8,128)(2,1)} %k_in.1, bf16[256,128]{1,0:T(8,128)(2,1)} %v_in.1, bf16[256,128]{1,0:T(8,128)(2,1)} %do_in.1), custom_call_target="tpu_custom_call" | custom-call | tf_op jit(solution)/shard_map/attention_backward/pallas_call | solution.py:374
  72.5 0.0 copy-start.1
  72.5 1.7 %copy.10 = bf16[256,512]{1,0:T(8,128)(2,1)} copy(bf16[256,512]{1,0:T(8,128)(2,1)} %get-tuple-element.6) | data formatting | bytes 524288
  74.2 0.0 copy-done.1
  74.2 0.0 copy-start
  74.2 0.7 copy.11
  74.9 0.3 copy-done
  75.3 0.7 copy.12
Async XLA Ops:
  72.5 1.7 %copy-start.1 = (bf16[256,512]{1,0:T(8,128)(2,1)S(1)}, bf16[256,512]{1,0:T(8,128)(2,1)}, u32[]{:S(2)}) copy-start(bf16[256,512]{1,0:T(8,128)(2,1)} %get-tuple-element.7) | copy-start | bytes 786436
  74.2 1.0 %copy-start = (bf16[256,512]{1,0:T(8,128)(2,1)S(1)}, bf16[256,512]{1,0:T(8,128)(2,1)}, u32[]{:S(2)}) copy-start(bf16[256,512]{1,0:T(8,128)(2,1)} %get-tuple-element.8) | copy-start | bytes 786436

commit v2 on v1

v2 whole, which is shorter than its diff:
```python
import math

import jax
import jax.numpy as jnp
from jax import lax
from jax.experimental import pallas as pl
from jax.experimental.pallas import tpu as pltpu
from jax.sharding import PartitionSpec as P

HEAD_DIM = 128
NZ, NX, NY = 8, 4, 2
NXY = NX * NY
NCORE = 2
SCALE = 1.0 / math.sqrt(HEAD_DIM)
LOG2E_SCALE = math.log2(math.e) * SCALE
MESH = pl.DeviceIdType.MESH
F32 = jnp.float32
BF16 = jnp.bfloat16
NT = (((1,), (1,)), ((), ()))
NN = (((1,), (0,)), ((), ()))


def dot(a, b, dims):
    return lax.dot_general(a, b, dims, preferred_element_type=F32)


Z_AT = [0, 1, -1, 2, -2, 3, -3, 4]
XY_AT = [(0, 0), (0, 1), (1, 0), (-1, 0), (1, 1), (-1, 1), (2, 0), (2, 1)]


def kernel(
    q_in,
    k_in,
    v_in,
    do_in,
    oq,
    ok,
    ov,
    qd,
    kv,
    scores,
    dprobs,
    probs_low,
    d_low,
    kt,
    qdf,
    st_own,
    st_all,
    lse,
    delta,
    factor,
    pkv,
    dq_own,
    xsend,
    xrecv,
    zsend,
    zrecv,
    ysum,
    yrecv,
    fin,
    fin_q,
    local_sem,
    send_sem,
    recv_sem,
):
    rows = q_in.shape[0]
    total_q = NZ * rows
    total_k = NXY * rows
    seq = lax.axis_index("seq")
    head = lax.axis_index("head")
    z = seq // NXY
    x = (seq // NY) % NX
    y = seq % NY

    def at(dz=0, dx=0, dy=0):
        zz = (z + dz + NZ) % NZ
        xx = (x + dx + NX) % NX
        yy = (y + dy) % NY
        return (zz * NXY + xx * NY + yy, head)

    def head_at(dh):
        return (seq, (head + dh) % (2 * NCORE))

    counter = [0]
    sent = []

    def remote(src, dst, device):
        i = counter[0]
        counter[0] += 1
        c = pltpu.make_async_remote_copy(
            src_ref=src,
            dst_ref=dst,
            send_sem=send_sem.at[i],
            recv_sem=recv_sem.at[i],
            device_id=device,
            device_id_type=MESH,
        )
        sent.append(c)
        return c

    own = [
        pltpu.make_async_copy(src, dst, local_sem.at[i])
        for i, (src, dst) in enumerate(
            [
                (q_in, qd.at[0, 0]),
                (do_in, qd.at[1, 0]),
                (k_in, kv.at[0, 0]),
                (v_in, kv.at[1, 0]),
            ]
        )
    ]
    for c in own:
        c.start()

    barrier = pltpu.get_barrier_semaphore()
    peers = [at(dz=d) for d in range(1, NZ)]
    peers += [at(dx=1), at(dx=-1), at(dy=1)]
    peers += [head_at(d) for d in range(1, 2 * NCORE)]
    for p in peers:
        pl.semaphore_signal(barrier, inc=1, device_id=p, device_id_type=MESH)
    for c in own:
        c.wait()
    pl.semaphore_wait(barrier, len(peers))

    zc = {}
    for part in range(2):
        zc[2, part] = remote(qd.at[part, 0], qd.at[part, 2], at(dz=1))
        zc[1, part] = remote(qd.at[part, 0], qd.at[part, 1], at(dz=-1))
    kc = {}
    for part in range(2):
        kc[3, part] = remote(kv.at[part, 0], kv.at[part, 3], at(dx=1))
        kc[2, part] = remote(kv.at[part, 0], kv.at[part, 2], at(dx=-1))
        kc[1, part] = remote(kv.at[part, 0], kv.at[part, 1], at(dy=1))
    for part in range(2):
        for c in (zc[2, part], zc[1, part], kc[3, part], kc[2, part], kc[1, part]):
            c.start()

    def z_forward(a, part):
        zc[a, part].wait_recv()
        b = a + 2
        if b < 7:
            zc[b, part] = remote(
                qd.at[part, a], qd.at[part, b], at(dz=-1 if a % 2 else 1)
            )
            zc[b, part].start()
        elif (a == 6) == (part == 0):
            zc[7, part] = remote(
                qd.at[part, a], qd.at[part, 7], at(dz=-1 if a % 2 else 1)
            )
            zc[7, part].start()

    for part in range(2):
        z_forward(2, part)
        z_forward(1, part)
        kc[1, part].wait_recv()
        kc[5, part] = remote(kv.at[part, 1], kv.at[part, 5], at(dx=1))
        kc[4, part] = remote(kv.at[part, 1], kv.at[part, 4], at(dx=-1))
        kc[5, part].start()
        kc[4, part].start()
        kc[3, part].wait_recv()
        kc[2, part].wait_recv()
        if part == 0:
            kc[6, 0] = remote(kv.at[0, 3], kv.at[0, 6], at(dx=1))
            kc[6, 0].start()
        else:
            kc[6, 1] = remote(kv.at[1, 2], kv.at[1, 6], at(dx=-1))
            kc[6, 1].start()
    for part in range(2):
        z_forward(4, part)
        z_forward(3, part)
    for part in range(2):
        kc[6, part].wait_recv()
        kc[7, part] = remote(kv.at[part, 6], kv.at[part, 7], at(dy=1))
        kc[7, part].start()
    for part in range(2):
        z_forward(6, part)
        z_forward(5, part)
    for part in range(2):
        kc[5, part].wait_recv()
        kc[4, part].wait_recv()
    for part in range(2):
        kc[7, part].wait_recv()
    for part in range(2):
        zc[7, part].wait_recv()

    qb = 2 * rows
    nq = NZ // 2
    st_base = counter[0]
    counter[0] += nq * (NZ - 1)

    def stat_copy(i, d):
        k = st_base + i * (NZ - 1) + d - 1
        return pltpu.make_async_remote_copy(
            src_ref=st_own.at[i],
            dst_ref=st_all.at[d, i],
            send_sem=send_sem.at[k],
            recv_sem=recv_sem.at[k],
            device_id=at(dz=d),
            device_id_type=MESH,
        )

    @pl.loop(0, nq)
    def _(i):
        qs = pl.ds(pl.multiple_of(i * qb, qb), qb)
        two = pl.ds(pl.multiple_of(i * 2, 2), 2)
        qq = qd[0, two].reshape(qb, HEAD_DIM)
        dd = qd[1, two].reshape(qb, HEAD_DIM)
        s = dot(kv[0].reshape(total_k, HEAD_DIM), qq, NT)
        scores[:, qs] = s
        m = jnp.max(s, axis=0, keepdims=True) * LOG2E_SCALE
        e = jnp.exp2(s * LOG2E_SCALE - m)
        dp = dot(kv[1].reshape(total_k, HEAD_DIM), dd, NT)
        dprobs[:, qs] = dp
        l = jnp.sum(e, axis=0, keepdims=True)
        w = jnp.sum(e * dp, axis=0, keepdims=True)
        top = m + jnp.log2(l)
        w = w / l
        lse[:, qs] = top
        for r in range(4):
            st_own[i, pl.ds(r, 1), :] = top[:, r * 128 : (r + 1) * 128]
            st_own[i, pl.ds(4 + r, 1), :] = w[:, r * 128 : (r + 1) * 128]
        for d in range(1, NZ):
            stat_copy(i, d).start()

    for j in range(NXY):
        kt[:, pl.ds(j * rows, rows)] = kv[0, j].T

    @pl.loop(0, NXY)
    def _(j):
        ks = pl.ds(pl.multiple_of(j * rows, rows), rows)
        p = jnp.exp2(scores[ks, :] * LOG2E_SCALE - lse[...])
        scores[ks, :] = p
        probs_low[ks, :] = p.astype(BF16)

    st_all[0] = st_own[...]
    for i in range(nq):
        for d in range(1, NZ):
            stat_copy(i, d).wait_recv()
    for slot, dz in enumerate(Z_AT):
        tops, deltas = [], []
        for d in range(NZ):
            there = Z_AT.index((dz + d + 3) % NZ - 3)
            i, b = there // 2, there % 2
            tops.append(st_all[d, i, pl.ds(2 * b, 2), :])
            deltas.append(st_all[d, i, pl.ds(4 + 2 * b, 2), :])
        big = tops[0]
        for t in tops[1:]:
            big = jnp.maximum(big, t)
        mass = jnp.zeros_like(big)
        weighted = jnp.zeros_like(big)
        for t, w in zip(tops, deltas):
            f = jnp.exp2(t - big)
            mass += f
            weighted += f * w
        weighted = weighted / mass
        own_factor = jnp.exp2(tops[0] - (big + jnp.log2(mass)))
        for r in range(2):
            cols = pl.ds(slot * rows + r * 128, 128)
            delta[:, cols] = weighted[r : r + 1, :]
            factor[:, cols] = own_factor[r : r + 1, :]
        wide = jnp.broadcast_to(
            factor[:, pl.ds(slot * rows, rows)], (HEAD_DIM, rows)
        ).T
        for part in range(2):
            qdf[part, slot] = (qd[part, slot].astype(F32) * wide).astype(BF16)

    xc = {}
    for part in (1, 0):
        for slot in range(2, NXY):
            dx, dy = XY_AT[slot]
            xc[part, slot] = remote(
                xsend.at[part, slot], xrecv.at[part, slot], at(dx=dx)
            )
    zc2 = {
        slot: remote(zsend.at[slot], zrecv.at[slot], at(dz=Z_AT[slot]))
        for slot in range(1, NZ)
    }

    def key_side(part, left):
        @pl.loop(0, NXY)
        def _(it):
            slot = NXY - 1 - it
            ks = pl.ds(pl.multiple_of(slot * rows, rows), rows)
            t = dot(left[ks, :], qdf[part].reshape(total_q, HEAD_DIM), NN)
            if part == 0:
                t = t * SCALE
            xsend[part, slot] = t.astype(BF16)

            @pl.when(slot < 2)
            def _():
                pkv[part, jnp.minimum(slot, 1)] = t

            for s in range(2, NXY):

                @pl.when(slot == s)
                def _():
                    xc[part, s].start()

    key_side(1, probs_low)

    @pl.loop(0, nq)
    def _(it):
        i = nq - 1 - it
        qs = pl.ds(pl.multiple_of(i * qb, qb), qb)
        ds = (scores[:, qs] * (dprobs[:, qs] - delta[:, qs])).astype(BF16)
        d_low[:, qs] = ds
        t = dot(kt[...], ds, NN) * (factor[:, qs] * SCALE)
        for b in range(2):
            mine = t[:, b * rows : (b + 1) * rows].T
            zsend[i * 2 + b] = mine.astype(BF16)

            @pl.when(i * 2 + b == 0)
            def _():
                dq_own[...] = mine

        for s in range(NZ):
            if s:

                @pl.when(i == s // 2)
                def _():
                    zc2[s].start()

    key_side(0, d_low)

    def up(ref):
        return ref.astype(F32)

    yc = {}

    def over_x(part):
        for dy in (1, 0):
            total = pkv[part, dy]
            for slot in range(2, NXY):
                if XY_AT[slot][1] == dy:
                    xc[part, slot].wait_recv()
                    total += up(xrecv[part, slot])
            ysum[part, dy] = total.astype(BF16)
            seq_to, _ = at(dy=dy)
            far = (head + NCORE) % (2 * NCORE)
            if dy:
                yc[part, 0] = remote(
                    ysum.at[part, 1], yrecv.at[part, 0], (seq_to, head)
                )
                yc[part, 0].start()
            yc[part, 1 + dy] = remote(
                ysum.at[part, dy], yrecv.at[part, 1 + dy], (seq_to, far)
            )
            yc[part, 1 + dy].start()

    def columns(out, h):
        return out.at[
            :, pl.ds(pl.multiple_of(h * HEAD_DIM, HEAD_DIM), HEAD_DIM)
        ]

    ends = []
    other = head + 1 - 2 * (head % 2)

    def over_y(part, out):
        yc[part, 0].wait_recv()
        fin[part, 0] = (up(ysum[part, 0]) + up(yrecv[part, 0])).astype(BF16)
        yc[part, 1].wait_recv()
        yc[part, 2].wait_recv()
        fin[part, 1] = (up(yrecv[part, 1]) + up(yrecv[part, 2])).astype(BF16)
        for b in range(2):
            cols = columns(out, (head + NCORE * b) % (2 * NCORE))
            c = remote(fin.at[part, b], cols, (seq, other))
            c.start()
            ends.append(c.wait_recv)
            c = pltpu.make_async_copy(fin.at[part, b], cols, local_sem.at[2 * part + b])
            c.start()
            ends.append(c.wait)

    over_x(1)
    over_x(0)
    over_y(1, ov)
    total = dq_own[...]
    for slot in range(1, NZ):
        zc2[slot].wait_recv()
        total += up(zrecv[slot])
    fin_q[...] = total.astype(BF16)
    cols = columns(oq, head)
    for d in range(1, 2 * NCORE):
        c = remote(fin_q, cols, head_at(d))
        c.start()
        ends.append(c.wait_recv)
    c = pltpu.make_async_copy(fin_q, cols, local_sem.at[4])
    c.start()
    ends.append(c.wait)
    over_y(0, ok)
    for wait in ends:
        wait()
    for c in sent:
        c.wait_send()
    for i in range(nq):
        for d in range(1, NZ):
            stat_copy(i, d).wait_send()


def local(queries, keys, values, d_out):
    rows, width = queries.shape
    total = NZ * rows
    any_spec = pl.BlockSpec(memory_space=pl.ANY)
    out = jax.ShapeDtypeStruct((rows, 2 * NCORE * width), BF16)
    vm = pltpu.VMEM
    return pl.pallas_call(
        kernel,
        out_shape=[out, out, out],
        in_specs=[any_spec] * 4,
        out_specs=[any_spec] * 3,
        scratch_shapes=[
            vm((2, NZ, rows, width), BF16),
            vm((2, NXY, rows, width), BF16),
            vm((total, total), F32),
            vm((total, total), F32),
            vm((total, total), BF16),
            vm((total, total), BF16),
            vm((width, total), BF16),
            vm((2, NZ, rows, width), BF16),
            vm((NZ // 2, 8, 128), F32),
            vm((NZ, NZ // 2, 8, 128), F32),
            vm((1, total), F32),
            vm((1, total), F32),
            vm((1, total), F32),
            vm((2, 2, rows, width), F32),
            vm((rows, width), F32),
            vm((2, NXY, rows, width), BF16),
            vm((2, NXY, rows, width), BF16),
            vm((NZ, rows, width), BF16),
            vm((NZ, rows, width), BF16),
            vm((2, 2, rows, width), BF16),
            vm((2, 3, rows, width), BF16),
            vm((2, 2, rows, width), BF16),
            vm((rows, width), BF16),
            pltpu.SemaphoreType.DMA((5,)),
            pltpu.SemaphoreType.DMA((112,)),
            pltpu.SemaphoreType.DMA((112,)),
        ],
        compiler_params=pltpu.CompilerParams(
            collective_id=0, has_side_effects=True, vmem_limit_bytes=62 * 2**20
        ),
        name="attention_backward",
    )(queries, keys, values, d_out)


def solution(mesh):
    in_specs = (P("seq", "head"), P("seq", "head"), P("seq", "head"), P("seq", "head"))
    out_specs = (P("seq", None), P("seq", None), P("seq", None))
    return jax.shard_map(local, mesh=mesh, in_specs=in_specs, out_specs=out_specs, check_vma=False)
```

time: 76.2 us -> 67 us (0.88)
  Pallas kernels: 71.9 us -> 62.7 us
    pallas_call x1, Pallas kernels: 71.9 us -> 62.7 us  [local(): pl.pallas_call(kernel, out_shape=[out, out, out], in_specs=[any_spec] * 4...]
where the time goes in v2:
time: 67 us; the launch traced here: 66.8 us
  Pallas kernels  62.7 us (94%)
  local copies, waits for them, and re-layouts  3.46 us (5%)
    pallas_call x1, Pallas kernels, local(): pl.pallas_call(kernel, out_shape=[out, out, out], in_specs=[any_spec] * 4...  62.7 us
    unnamed x7, local copies, waits for them, and re-layouts  3.46 us

profile of v2, /device:TPU:1, one launch (start us, length us, event | category | flops | bytes accessed | tf_op | source)
XLA Modules:
  0.0 66.8 jit_solution(17916686006216152403)
XLA Ops:
  0.6 62.7 %attention_backward.1 = (bf16[256,512]{1,0:T(8,128)(2,1)}, bf16[256,512]{1,0:T(8,128)(2,1)}, bf16[256,512]{1,0:T(8,128)(2,1)}) custom-call(bf16[256,128]{1,0:T(8,128)(2,1)} %q_in.1, bf16[256,128]{1,0:T(8,128)(2,1)} %k_in.1, bf16[256,128]{1,0:T(8,128)(2,1)} %v_in.1, bf16[256,128]{1,0:T(8,128)(2,1)} %do_in.1), custom_call_target="tpu_custom_call" | custom-call | tf_op jit(solution)/shard_map/attention_backward/pallas_call | solution.py:405
  63.3 0.0 copy-start.1
  63.3 1.7 %copy.10 = bf16[256,512]{1,0:T(8,128)(2,1)} copy(bf16[256,512]{1,0:T(8,128)(2,1)} %get-tuple-element.6) | data formatting | bytes 524288
  65.0 0.0 copy-done.1
  65.0 0.0 copy-start
  65.0 0.7 %copy.11 = bf16[256,512]{1,0:T(8,128)(2,1)} copy(bf16[256,512]{1,0:T(8,128)(2,1)S(1)} %copy-done.1) | data formatting | bytes 524288
  65.7 0.3 copy-done
  66.1 0.7 %copy.12 = bf16[256,512]{1,0:T(8,128)(2,1)} copy(bf16[256,512]{1,0:T(8,128)(2,1)S(1)} %copy-done) | data formatting | bytes 524288
Async XLA Ops:
  63.3 1.7 %copy-start.1 = (bf16[256,512]{1,0:T(8,128)(2,1)S(1)}, bf16[256,512]{1,0:T(8,128)(2,1)}, u32[]{:S(2)}) copy-start(bf16[256,512]{1,0:T(8,128)(2,1)} %get-tuple-element.7) | copy-start | bytes 786436
  65.0 1.0 %copy-start = (bf16[256,512]{1,0:T(8,128)(2,1)S(1)}, bf16[256,512]{1,0:T(8,128)(2,1)}, u32[]{:S(2)}) copy-start(bf16[256,512]{1,0:T(8,128)(2,1)} %get-tuple-element.8) | copy-start | bytes 786436

commit v3 on v2

--- a/solution.py
+++ b/solution.py
@@ -113,8 +113,7 @@
         c.start()
 
     barrier = pltpu.get_barrier_semaphore()
-    peers = [at(dz=d) for d in range(1, NZ)]
-    peers += [at(dx=1), at(dx=-1), at(dy=1)]
+    peers = [at(dz=1), at(dz=-1), at(dx=1), at(dx=-1), at(dx=2), at(dy=1)]
     peers += [head_at(d) for d in range(1, 2 * NCORE)]
     for p in peers:
         pl.semaphore_signal(barrier, inc=1, device_id=p, device_id_type=MESH)
@@ -122,69 +121,44 @@
         c.wait()
     pl.semaphore_wait(barrier, len(peers))
 
-    zc = {}
-    for part in range(2):
-        zc[2, part] = remote(qd.at[part, 0], qd.at[part, 2], at(dz=1))
-        zc[1, part] = remote(qd.at[part, 0], qd.at[part, 1], at(dz=-1))
-    kc = {}
-    for part in range(2):
-        kc[3, part] = remote(kv.at[part, 0], kv.at[part, 3], at(dx=1))
-        kc[2, part] = remote(kv.at[part, 0], kv.at[part, 2], at(dx=-1))
-        kc[1, part] = remote(kv.at[part, 0], kv.at[part, 1], at(dy=1))
-    for part in range(2):
-        for c in (zc[2, part], zc[1, part], kc[3, part], kc[2, part], kc[1, part]):
-            c.start()
-
-    def z_forward(a, part):
-        zc[a, part].wait_recv()
-        b = a + 2
-        if b < 7:
-            zc[b, part] = remote(
-                qd.at[part, a], qd.at[part, b], at(dz=-1 if a % 2 else 1)
-            )
-            zc[b, part].start()
-        elif (a == 6) == (part == 0):
-            zc[7, part] = remote(
-                qd.at[part, a], qd.at[part, 7], at(dz=-1 if a % 2 else 1)
-            )
-            zc[7, part].start()
-
-    for part in range(2):
-        z_forward(2, part)
-        z_forward(1, part)
-        kc[1, part].wait_recv()
-        kc[5, part] = remote(kv.at[part, 1], kv.at[part, 5], at(dx=1))
-        kc[4, part] = remote(kv.at[part, 1], kv.at[part, 4], at(dx=-1))
-        kc[5, part].start()
-        kc[4, part].start()
-        kc[3, part].wait_recv()
-        kc[2, part].wait_recv()
-        if part == 0:
-            kc[6, 0] = remote(kv.at[0, 3], kv.at[0, 6], at(dx=1))
-            kc[6, 0].start()
-        else:
-            kc[6, 1] = remote(kv.at[1, 2], kv.at[1, 6], at(dx=-1))
-            kc[6, 1].start()
-    for part in range(2):
-        z_forward(4, part)
-        z_forward(3, part)
-    for part in range(2):
-        kc[6, part].wait_recv()
-        kc[7, part] = remote(kv.at[part, 6], kv.at[part, 7], at(dy=1))
-        kc[7, part].start()
-    for part in range(2):
-        z_forward(6, part)
-        z_forward(5, part)
-    for part in range(2):
-        kc[5, part].wait_recv()
-        kc[4, part].wait_recv()
-    for part in range(2):
-        kc[7, part].wait_recv()
-    for part in range(2):
-        zc[7, part].wait_recv()
-
     qb = 2 * rows
     nq = NZ // 2
+    half = rows // 2
+    zc, kc = {}, {}
+
+    def z_send(a, b, part, h):
+        rs = pl.ds(h * half, half)
+        c = remote(qd.at[part, a, rs], qd.at[part, b, rs], at(dz=-1 if b in (1, 3, 5) or (b == 7 and part) else 1))
+        zc[b, part, h] = c
+        c.start()
+
+    def z_round(a, h_part, h):
+        zc[a, h_part, h].wait_recv()
+        if a < 6:
+            z_send(a, a + 2, h_part, h)
+        elif h_part == 0:
+            z_send(a, 7, h_part, h)
+        zc[a - 1, h_part, h].wait_recv()
+        if a < 6:
+            z_send(a - 1, a + 1, h_part, h)
+        elif h_part == 1:
+            z_send(a - 1, 7, h_part, h)
+
+    def k_send(a, b, part, device):
+        c = remote(kv.at[part, a], kv.at[part, b], device)
+        kc[b, part] = c
+        c.start()
+
+    for part in range(2):
+        for h in range(2):
+            z_send(0, 2, part, h)
+            z_send(0, 1, part, h)
+        k_send(0, 1, part, at(dy=1))
+        k_send(0, 3, part, at(dx=1))
+        k_send(0, 2, part, at(dx=-1))
+    for part in range(2):
+        k_send(0, 6, part, at(dx=2))
+
     st_base = counter[0]
     counter[0] += nq * (NZ - 1)
 
@@ -199,28 +173,78 @@
             device_id_type=MESH,
         )
 
-    @pl.loop(0, nq)
-    def _(i):
+    def block(i, k0, kn):
+        first, last = k0 == 0, k0 + kn == NXY
         qs = pl.ds(pl.multiple_of(i * qb, qb), qb)
+        ks = pl.ds(k0 * rows, kn * rows)
         two = pl.ds(pl.multiple_of(i * 2, 2), 2)
         qq = qd[0, two].reshape(qb, HEAD_DIM)
         dd = qd[1, two].reshape(qb, HEAD_DIM)
-        s = dot(kv[0].reshape(total_k, HEAD_DIM), qq, NT)
-        scores[:, qs] = s
+        s = dot(kv[0, pl.ds(k0, kn)].reshape(kn * rows, HEAD_DIM), qq, NT)
+        scores[ks, qs] = s
         m = jnp.max(s, axis=0, keepdims=True) * LOG2E_SCALE
+        if not first:
+            old = lse[:, qs]
+            m = jnp.maximum(m, old)
         e = jnp.exp2(s * LOG2E_SCALE - m)
-        dp = dot(kv[1].reshape(total_k, HEAD_DIM), dd, NT)
-        dprobs[:, qs] = dp
+        dp = dot(kv[1, pl.ds(k0, kn)].reshape(kn * rows, HEAD_DIM), dd, NT)
+        dprobs[ks, qs] = dp
         l = jnp.sum(e, axis=0, keepdims=True)
         w = jnp.sum(e * dp, axis=0, keepdims=True)
-        top = m + jnp.log2(l)
-        w = w / l
-        lse[:, qs] = top
-        for r in range(4):
-            st_own[i, pl.ds(r, 1), :] = top[:, r * 128 : (r + 1) * 128]
-            st_own[i, pl.ds(4 + r, 1), :] = w[:, r * 128 : (r + 1) * 128]
-        for d in range(1, NZ):
-            stat_copy(i, d).start()
+        if not first:
+            fade = jnp.exp2(old - m)
+            l += fade * factor[:, qs]
+            w += fade * delta[:, qs]
+        if last:
+            m = m + jnp.log2(l)
+            w = w / l
+            for r in range(4):
+                st_own[i, pl.ds(r, 1), :] = m[:, r * 128 : (r + 1) * 128]
+                st_own[i, pl.ds(4 + r, 1), :] = w[:, r * 128 : (r + 1) * 128]
+            for d in range(1, NZ):
+                stat_copy(i, d).start()
+        else:
+            factor[:, qs] = l
+            delta[:, qs] = w
+        lse[:, qs] = m
+
+    def spread(part):
+        kc[1, part].wait_recv()
+        k_send(1, 5, part, at(dx=1))
+        k_send(1, 4, part, at(dx=-1))
+
+    z_round(2, 0, 0)
+    z_round(2, 0, 1)
+    spread(0)
+    z_round(2, 1, 0)
+    z_round(2, 1, 1)
+    spread(1)
+    for part in range(2):
+        kc[2, part].wait_recv()
+        kc[3, part].wait_recv()
+    block(0, 0, NXY // 2)
+    for part in range(2):
+        kc[6, part].wait_recv()
+        k_send(6, 7, part, at(dy=1))
+        z_round(4, part, 0)
+        z_round(4, part, 1)
+    block(1, 0, NXY // 2)
+    for part in range(2):
+        z_round(6, part, 0)
+        z_round(6, part, 1)
+    block(2, 0, NXY // 2)
+    for part in range(2):
+        for slot in (4, 5, 7):
+            kc[slot, part].wait_recv()
+
+    @pl.loop(0, nq - 1)
+    def _(i):
+        block(i, NXY // 2, NXY // 2)
+
+    for part in range(2):
+        for h in range(2):
+            zc[7, part, h].wait_recv()
+    block(nq - 1, 0, NXY)
 
     for j in range(NXY):
         kt[:, pl.ds(j * rows, rows)] = kv[0, j].T
@@ -276,51 +300,55 @@
         for slot in range(1, NZ)
     }
 
-    def key_side(part, left):
-        @pl.loop(0, NXY)
+    def key_side(part, left, high, low):
+        @pl.loop(0, high - low)
         def _(it):
-            slot = NXY - 1 - it
+            slot = high - 1 - it
             ks = pl.ds(pl.multiple_of(slot * rows, rows), rows)
             t = dot(left[ks, :], qdf[part].reshape(total_q, HEAD_DIM), NN)
             if part == 0:
                 t = t * SCALE
             xsend[part, slot] = t.astype(BF16)
-
-            @pl.when(slot < 2)
-            def _():
-                pkv[part, jnp.minimum(slot, 1)] = t
-
-            for s in range(2, NXY):
+            if low == 0:
+
+                @pl.when(slot < 2)
+                def _():
+                    pkv[part, jnp.minimum(slot, 1)] = t
+
+            for s in range(max(low, 2), high):
 
                 @pl.when(slot == s)
                 def _():
                     xc[part, s].start()
 
-    key_side(1, probs_low)
-
-    @pl.loop(0, nq)
-    def _(it):
-        i = nq - 1 - it
-        qs = pl.ds(pl.multiple_of(i * qb, qb), qb)
-        ds = (scores[:, qs] * (dprobs[:, qs] - delta[:, qs])).astype(BF16)
-        d_low[:, qs] = ds
-        t = dot(kt[...], ds, NN) * (factor[:, qs] * SCALE)
-        for b in range(2):
-            mine = t[:, b * rows : (b + 1) * rows].T
-            zsend[i * 2 + b] = mine.astype(BF16)
-
-            @pl.when(i * 2 + b == 0)
-            def _():
-                dq_own[...] = mine
-
-        for s in range(NZ):
-            if s:
+    def query_side(high, low):
+        @pl.loop(0, high - low)
+        def _(it):
+            i = high - 1 - it
+            qs = pl.ds(pl.multiple_of(i * qb, qb), qb)
+            ds = (scores[:, qs] * (dprobs[:, qs] - delta[:, qs])).astype(BF16)
+            d_low[:, qs] = ds
+            t = dot(kt[...], ds, NN) * (factor[:, qs] * SCALE)
+            for b in range(2):
+                mine = t[:, b * rows : (b + 1) * rows].T
+                zsend[i * 2 + b] = mine.astype(BF16)
+                if low == 0 and b == 0:
+
+                    @pl.when(i == 0)
+                    def _():
+                        dq_own[...] = mine
+
+            for s in range(max(2 * low, 1), 2 * high):
 
                 @pl.when(i == s // 2)
                 def _():
                     zc2[s].start()
 
-    key_side(0, d_low)
+    key_side(1, probs_low, 8, 6)
+    query_side(4, 2)
+    key_side(1, probs_low, 6, 0)
+    query_side(2, 0)
+    key_side(0, d_low, 8, 0)
 
     def up(ref):
         return ref.astype(F32)
@@ -396,13 +424,19 @@
             stat_copy(i, d).wait_send()
 
 
+def hand_over(a, b, c, oa, ob, oc):
+    oa[...] = a[...]
+    ob[...] = b[...]
+    oc[...] = c[...]
+
+
 def local(queries, keys, values, d_out):
     rows, width = queries.shape
     total = NZ * rows
     any_spec = pl.BlockSpec(memory_space=pl.ANY)
     out = jax.ShapeDtypeStruct((rows, 2 * NCORE * width), BF16)
     vm = pltpu.VMEM
-    return pl.pallas_call(
+    outs = pl.pallas_call(
         kernel,
         out_shape=[out, out, out],
         in_specs=[any_spec] * 4,
@@ -436,10 +470,18 @@
             pltpu.SemaphoreType.DMA((112,)),
         ],
         compiler_params=pltpu.CompilerParams(
-            collective_id=0, has_side_effects=True, vmem_limit_bytes=62 * 2**20
+            collective_id=0, has_side_effects=True, vmem_limit_bytes=63 * 2**20
         ),
         name="attention_backward",
     )(queries, keys, values, d_out)
+    spec = pl.BlockSpec(memory_space=pltpu.VMEM)
+    return pl.pallas_call(
+        hand_over,
+        out_shape=[out, out, out],
+        in_specs=[spec] * 3,
+        out_specs=[spec] * 3,
+        name="hand_over",
+    )(*outs)
 
 
 def solution(mesh):

time: 67 us -> 59 us (0.88)
  Pallas kernels: 62.7 us -> 58.2 us
  local copies, waits for them, and re-layouts: 3.46 us -> 0 us
    pallas_call x1, Pallas kernels: 62.7 us -> 56.2 us  [local(): pl.pallas_call(kernel, out_shape=[out, out, out], in_specs=[any_spec] * 4...]
    unnamed x7 -> x0, local copies, waits for them, and re-layouts: 3.46 us -> none
    pallas_call x0 -> x1, Pallas kernels: none -> 2 us  [local(): pl.pallas_call(hand_over, out_shape=[out, out, out], in_specs=[spec] * 3,...]
where the time goes in v3:
time: 59 us; the launch traced here: 58.9 us
  Pallas kernels  58.2 us (99%)
  between operations  0.64 us (1%)
    pallas_call x1, Pallas kernels, local(): pl.pallas_call(kernel, out_shape=[out, out, out], in_specs=[any_spec] * 4...  56.2 us
    pallas_call x1, Pallas kernels, local(): pl.pallas_call(hand_over, out_shape=[out, out, out], in_specs=[spec] * 3,...  2 us

profile of v3, /device:TPU:1, one launch (start us, length us, event | category | flops | bytes accessed | tf_op | source)
XLA Modules:
  0.0 58.9 jit_solution(4161520918776141673)
XLA Ops:
  0.6 56.2 %attention_backward.1 = (bf16[256,512]{1,0:T(8,128)(2,1)}, bf16[256,512]{1,0:T(8,128)(2,1)}, bf16[256,512]{1,0:T(8,128)(2,1)}) custom-call(bf16[256,128]{1,0:T(8,128)(2,1)} %q_in.1, bf16[256,128]{1,0:T(8,128)(2,1)} %k_in.1, bf16[256,128]{1,0:T(8,128)(2,1)} %v_in.1, bf16[256,128]{1,0:T(8,128)(2,1)} %do_in.1), custom_call_target="tpu_custom_call" | custom-call | tf_op jit(solution)/shard_map/attention_backward/pallas_call | solution.py:439
  56.9 2.0 %hand_over.1 = (bf16[256,512]{1,0:T(8,128)(2,1)}, bf16[256,512]{1,0:T(8,128)(2,1)}, bf16[256,512]{1,0:T(8,128)(2,1)}) custom-call(bf16[256,512]{1,0:T(8,128)(2,1)} %get-tuple-element.6.a, bf16[256,512]{1,0:T(8,128)(2,1)} %get-tuple-element.7.b, bf16[256,512]{1,0:T(8,128)(2,1)} %get-tuple-element.8.c), custom_call_target="tpu_custom_call" | custom-call | tf_op jit(solution)/shard_map/hand_over/pallas_call | solution.py:478

commit v4 on v3

--- a/solution.py
+++ b/solution.py
@@ -25,7 +25,7 @@
 
 
 Z_AT = [0, 1, -1, 2, -2, 3, -3, 4]
-XY_AT = [(0, 0), (0, 1), (1, 0), (-1, 0), (1, 1), (-1, 1), (2, 0), (2, 1)]
+XY_AT = [(0, 0), (0, 1), (1, 0), (-1, 0), (2, 0), (1, 1), (-1, 1), (2, 1)]
 
 
 def kernel(
@@ -126,23 +126,22 @@
     half = rows // 2
     zc, kc = {}, {}
 
-    def z_send(a, b, part, h):
+    def z_send(a, b, part, h, dz):
         rs = pl.ds(h * half, half)
-        c = remote(qd.at[part, a, rs], qd.at[part, b, rs], at(dz=-1 if b in (1, 3, 5) or (b == 7 and part) else 1))
+        c = remote(qd.at[part, a, rs], qd.at[part, b, rs], at(dz=dz))
         zc[b, part, h] = c
         c.start()
 
-    def z_round(a, h_part, h):
-        zc[a, h_part, h].wait_recv()
-        if a < 6:
-            z_send(a, a + 2, h_part, h)
-        elif h_part == 0:
-            z_send(a, 7, h_part, h)
-        zc[a - 1, h_part, h].wait_recv()
-        if a < 6:
-            z_send(a - 1, a + 1, h_part, h)
-        elif h_part == 1:
-            z_send(a - 1, 7, h_part, h)
+    def z_round(a, part, h):
+        zc[a, part, h].wait_recv()
+        z_send(a, a + 2, part, h, 1)
+        zc[a - 1, part, h].wait_recv()
+        z_send(a - 1, a + 1, part, h, -1)
+        if a == 4:
+            if part == 0:
+                z_send(4, 7, part, h, 2)
+            else:
+                z_send(3, 7, part, h, -2)
 
     def k_send(a, b, part, device):
         c = remote(kv.at[part, a], kv.at[part, b], device)
@@ -151,35 +150,37 @@
 
     for part in range(2):
         for h in range(2):
-            z_send(0, 2, part, h)
-            z_send(0, 1, part, h)
+            z_send(0, 2, part, h, 1)
+            z_send(0, 1, part, h, -1)
         k_send(0, 1, part, at(dy=1))
         k_send(0, 3, part, at(dx=1))
         k_send(0, 2, part, at(dx=-1))
     for part in range(2):
-        k_send(0, 6, part, at(dx=2))
-
+        k_send(0, 4, part, at(dx=2))
+
+    groups = ((0, 5), (5, 2), (7, 1))
     st_base = counter[0]
-    counter[0] += nq * (NZ - 1)
-
-    def stat_copy(i, d):
-        k = st_base + i * (NZ - 1) + d - 1
+    counter[0] += len(groups) * (NZ - 1)
+
+    def stat_copy(g, d):
+        k = st_base + g * (NZ - 1) + d - 1
+        slots = pl.ds(*groups[g])
         return pltpu.make_async_remote_copy(
-            src_ref=st_own.at[i],
-            dst_ref=st_all.at[d, i],
+            src_ref=st_own.at[slots],
+            dst_ref=st_all.at[d, slots],
             send_sem=send_sem.at[k],
             recv_sem=recv_sem.at[k],
             device_id=at(dz=d),
             device_id_type=MESH,
         )
 
-    def block(i, k0, kn):
+    def block(c0, cn, k0, kn):
         first, last = k0 == 0, k0 + kn == NXY
-        qs = pl.ds(pl.multiple_of(i * qb, qb), qb)
+        qs = pl.ds(c0 * rows, cn * rows)
         ks = pl.ds(k0 * rows, kn * rows)
-        two = pl.ds(pl.multiple_of(i * 2, 2), 2)
-        qq = qd[0, two].reshape(qb, HEAD_DIM)
-        dd = qd[1, two].reshape(qb, HEAD_DIM)
+        slots = pl.ds(c0, cn)
+        qq = qd[0, slots].reshape(cn * rows, HEAD_DIM)
+        dd = qd[1, slots].reshape(cn * rows, HEAD_DIM)
         s = dot(kv[0, pl.ds(k0, kn)].reshape(kn * rows, HEAD_DIM), qq, NT)
         scores[ks, qs] = s
         m = jnp.max(s, axis=0, keepdims=True) * LOG2E_SCALE
@@ -198,11 +199,11 @@
         if last:
             m = m + jnp.log2(l)
             w = w / l
-            for r in range(4):
-                st_own[i, pl.ds(r, 1), :] = m[:, r * 128 : (r + 1) * 128]
-                st_own[i, pl.ds(4 + r, 1), :] = w[:, r * 128 : (r + 1) * 128]
-            for d in range(1, NZ):
-                stat_copy(i, d).start()
+            for c in range(cn):
+                for r in range(2):
+                    lanes = slice((2 * c + r) * 128, (2 * c + r + 1) * 128)
+                    st_own[c0 + c, pl.ds(r, 1), :] = m[:, lanes]
+                    st_own[c0 + c, pl.ds(2 + r, 1), :] = w[:, lanes]
         else:
             factor[:, qs] = l
             delta[:, qs] = w
@@ -210,41 +211,54 @@
 
     def spread(part):
         kc[1, part].wait_recv()
-        k_send(1, 5, part, at(dx=1))
-        k_send(1, 4, part, at(dx=-1))
+        k_send(1, 6, part, at(dx=1))
+        k_send(1, 5, part, at(dx=-1))
+
+    def far_keys(part):
+        kc[4, part].wait_recv()
+        k_send(4, 7, part, at(dy=1))
 
     z_round(2, 0, 0)
     z_round(2, 0, 1)
+    z_round(2, 1, 0)
     spread(0)
-    z_round(2, 1, 0)
     z_round(2, 1, 1)
     spread(1)
     for part in range(2):
         kc[2, part].wait_recv()
         kc[3, part].wait_recv()
-    block(0, 0, NXY // 2)
+    block(0, 3, 0, 4)
+    z_round(4, 0, 0)
+    z_round(4, 0, 1)
+    far_keys(0)
+    z_round(4, 1, 0)
+    z_round(4, 1, 1)
+    far_keys(1)
+    block(3, 2, 0, 4)
     for part in range(2):
+        kc[5, part].wait_recv()
         kc[6, part].wait_recv()
-        k_send(6, 7, part, at(dy=1))
-        z_round(4, part, 0)
-        z_round(4, part, 1)
-    block(1, 0, NXY // 2)
+    block(0, 3, 4, 3)
+    block(3, 2, 4, 3)
+    kc[7, 0].wait_recv()
+    kc[7, 1].wait_recv()
+    block(0, 5, 7, 1)
     for part in range(2):
-        z_round(6, part, 0)
-        z_round(6, part, 1)
-    block(2, 0, NXY // 2)
-    for part in range(2):
-        for slot in (4, 5, 7):
-            kc[slot, part].wait_recv()
-
-    @pl.loop(0, nq - 1)
-    def _(i):
-        block(i, NXY // 2, NXY // 2)
-
+        for h in range(2):
+            zc[6, part, h].wait_recv()
+            zc[5, part, h].wait_recv()
+    for d in (1, 7, 2, 6, 3, 5):
+        stat_copy(0, d).start()
+    block(5, 2, 0, NXY)
     for part in range(2):
         for h in range(2):
             zc[7, part, h].wait_recv()
-    block(nq - 1, 0, NXY)
+    stat_copy(0, 4).start()
+    for d in (4, 3, 5, 2, 6, 1, 7):
+        stat_copy(1, d).start()
+    block(7, 1, 0, NXY)
+    for d in (4, 3, 5, 2, 6, 1, 7):
+        stat_copy(2, d).start()
 
     for j in range(NXY):
         kt[:, pl.ds(j * rows, rows)] = kv[0, j].T
@@ -257,16 +271,15 @@
         probs_low[ks, :] = p.astype(BF16)
 
     st_all[0] = st_own[...]
-    for i in range(nq):
+    for g in range(len(groups)):
         for d in range(1, NZ):
-            stat_copy(i, d).wait_recv()
+            stat_copy(g, d).wait_recv()
     for slot, dz in enumerate(Z_AT):
         tops, deltas = [], []
         for d in range(NZ):
             there = Z_AT.index((dz + d + 3) % NZ - 3)
-            i, b = there // 2, there % 2
-            tops.append(st_all[d, i, pl.ds(2 * b, 2), :])
-            deltas.append(st_all[d, i, pl.ds(4 + 2 * b, 2), :])
+            tops.append(st_all[d, there, pl.ds(0, 2), :])
+            deltas.append(st_all[d, there, pl.ds(2, 2), :])
         big = tops[0]
         for t in tops[1:]:
             big = jnp.maximum(big, t)
@@ -301,24 +314,26 @@
     }
 
     def key_side(part, left, high, low):
-        @pl.loop(0, high - low)
+        @pl.loop(0, (high - low) // 2)
         def _(it):
-            slot = high - 1 - it
-            ks = pl.ds(pl.multiple_of(slot * rows, rows), rows)
+            slot = high - 2 - 2 * it
+            ks = pl.ds(pl.multiple_of(slot * rows, rows), 2 * rows)
             t = dot(left[ks, :], qdf[part].reshape(total_q, HEAD_DIM), NN)
             if part == 0:
                 t = t * SCALE
-            xsend[part, slot] = t.astype(BF16)
+            t = t.reshape(2, rows, HEAD_DIM)
             if low == 0:
 
-                @pl.when(slot < 2)
+                @pl.when(slot == 0)
                 def _():
-                    pkv[part, jnp.minimum(slot, 1)] = t
-
-            for s in range(max(low, 2), high):
+                    pkv[part] = t
+
+            xsend[part, pl.ds(slot, 2)] = t.astype(BF16)
+            for s in range(max(low, 2), high, 2):
 
                 @pl.when(slot == s)
                 def _():
+                    xc[part, s + 1].start()
                     xc[part, s].start()
 
     def query_side(high, low):
@@ -344,11 +359,11 @@
                 def _():
                     zc2[s].start()
 
-    key_side(1, probs_low, 8, 6)
-    query_side(4, 2)
-    key_side(1, probs_low, 6, 0)
-    query_side(2, 0)
-    key_side(0, d_low, 8, 0)
+    key_side(1, probs_low, 8, 2)
+    query_side(4, 0)
+    key_side(0, d_low, 8, 2)
+    key_side(1, probs_low, 2, 0)
+    key_side(0, d_low, 2, 0)
 
     def up(ref):
         return ref.astype(F32)
@@ -419,9 +434,9 @@
         wait()
     for c in sent:
         c.wait_send()
-    for i in range(nq):
+    for g in range(len(groups)):
         for d in range(1, NZ):
-            stat_copy(i, d).wait_send()
+            stat_copy(g, d).wait_send()
 
 
 def hand_over(a, b, c, oa, ob, oc):
@@ -450,8 +465,8 @@
             vm((total, total), BF16),
             vm((width, total), BF16),
             vm((2, NZ, rows, width), BF16),
-            vm((NZ // 2, 8, 128), F32),
-            vm((NZ, NZ // 2, 8, 128), F32),
+            vm((NZ, 4, 128), F32),
+            vm((NZ, NZ, 4, 128), F32),
             vm((1, total), F32),
             vm((1, total), F32),
             vm((1, total), F32),

time: 59 us -> 56.5 us (0.958)
  Pallas kernels: 58.2 us -> 55.7 us
    pallas_call x1, Pallas kernels: 56.2 us -> 53.7 us  [local(): pl.pallas_call(kernel, out_shape=[out, out, out], in_specs=[any_spec] * 4...]
where the time goes in v4:
time: 56.5 us; the launch traced here: 56.3 us
  Pallas kernels  55.7 us (99%)
  between operations  0.64 us (1%)
    pallas_call x1, Pallas kernels, local(): pl.pallas_call(kernel, out_shape=[out, out, out], in_specs=[any_spec] * 4...  53.7 us
    pallas_call x1, Pallas kernels, local(): pl.pallas_call(hand_over, out_shape=[out, out, out], in_specs=[spec] * 3,...  2 us

profile of v4, /device:TPU:1, one launch (start us, length us, event | category | flops | bytes accessed | tf_op | source)
XLA Modules:
  0.0 56.3 jit_solution(10577005984783954151)
XLA Ops:
  0.6 53.7 %attention_backward.1 = (bf16[256,512]{1,0:T(8,128)(2,1)}, bf16[256,512]{1,0:T(8,128)(2,1)}, bf16[256,512]{1,0:T(8,128)(2,1)}) custom-call(bf16[256,128]{1,0:T(8,128)(2,1)} %q_in.1, bf16[256,128]{1,0:T(8,128)(2,1)} %k_in.1, bf16[256,128]{1,0:T(8,128)(2,1)} %v_in.1, bf16[256,128]{1,0:T(8,128)(2,1)} %do_in.1), custom_call_target="tpu_custom_call" | custom-call | tf_op jit(solution)/shard_map/attention_backward/pallas_call | solution.py:454
  54.3 2.0 %hand_over.1 = (bf16[256,512]{1,0:T(8,128)(2,1)}, bf16[256,512]{1,0:T(8,128)(2,1)}, bf16[256,512]{1,0:T(8,128)(2,1)}) custom-call(bf16[256,512]{1,0:T(8,128)(2,1)} %get-tuple-element.6.a, bf16[256,512]{1,0:T(8,128)(2,1)} %get-tuple-element.7.b, bf16[256,512]{1,0:T(8,128)(2,1)} %get-tuple-element.8.c), custom_call_target="tpu_custom_call" | custom-call | tf_op jit(solution)/shard_map/hand_over/pallas_call | solution.py:493

commit v5 on v4

--- a/solution.py
+++ b/solution.py
@@ -98,6 +98,10 @@
         sent.append(c)
         return c
 
+    def all_sent():
+        while sent:
+            sent.pop().wait_send()
+
     own = [
         pltpu.make_async_copy(src, dst, local_sem.at[i])
         for i, (src, dst) in enumerate(
@@ -227,13 +231,13 @@
     for part in range(2):
         kc[2, part].wait_recv()
         kc[3, part].wait_recv()
-    block(0, 3, 0, 4)
     z_round(4, 0, 0)
     z_round(4, 0, 1)
     far_keys(0)
     z_round(4, 1, 0)
     z_round(4, 1, 1)
     far_keys(1)
+    block(0, 3, 0, 4)
     block(3, 2, 0, 4)
     for part in range(2):
         kc[5, part].wait_recv()
@@ -269,6 +273,8 @@
         p = jnp.exp2(scores[ks, :] * LOG2E_SCALE - lse[...])
         scores[ks, :] = p
         probs_low[ks, :] = p.astype(BF16)
+
+    all_sent()
 
     st_all[0] = st_own[...]
     for g in range(len(groups)):
@@ -414,8 +420,11 @@
             ends.append(c.wait)
 
     over_x(1)
+    for g in range(len(groups)):
+        for d in range(1, NZ):
+            stat_copy(g, d).wait_send()
     over_x(0)
-    over_y(1, ov)
+    all_sent()
     total = dq_own[...]
     for slot in range(1, NZ):
         zc2[slot].wait_recv()
@@ -429,14 +438,11 @@
     c = pltpu.make_async_copy(fin_q, cols, local_sem.at[4])
     c.start()
     ends.append(c.wait)
+    over_y(1, ov)
     over_y(0, ok)
     for wait in ends:
         wait()
-    for c in sent:
-        c.wait_send()
-    for g in range(len(groups)):
-        for d in range(1, NZ):
-            stat_copy(g, d).wait_send()
+    all_sent()
 
 
 def hand_over(a, b, c, oa, ob, oc):

time: 56.5 us -> 55.8 us (0.988)
  Pallas kernels: 55.7 us -> 55 us
    pallas_call x1, Pallas kernels: 53.7 us -> 53 us  [local(): pl.pallas_call(kernel, out_shape=[out, out, out], in_specs=[any_spec] * 4...]
where the time goes in v5:
time: 55.8 us; the launch traced here: 55.6 us
  Pallas kernels  55 us (99%)
  between operations  0.64 us (1%)
    pallas_call x1, Pallas kernels, local(): pl.pallas_call(kernel, out_shape=[out, out, out], in_specs=[any_spec] * 4...  53 us
    pallas_call x1, Pallas kernels, local(): pl.pallas_call(hand_over, out_shape=[out, out, out], in_specs=[spec] * 3,...  2 us

profile of v5, /device:TPU:1, one launch (start us, length us, event | category | flops | bytes accessed | tf_op | source)
XLA Modules:
  0.0 55.6 jit_solution(10126047966185572308)
XLA Ops:
  0.6 53.0 %attention_backward.1 = (bf16[256,512]{1,0:T(8,128)(2,1)}, bf16[256,512]{1,0:T(8,128)(2,1)}, bf16[256,512]{1,0:T(8,128)(2,1)}) custom-call(bf16[256,128]{1,0:T(8,128)(2,1)} %q_in.1, bf16[256,128]{1,0:T(8,128)(2,1)} %k_in.1, bf16[256,128]{1,0:T(8,128)(2,1)} %v_in.1, bf16[256,128]{1,0:T(8,128)(2,1)} %do_in.1), custom_call_target="tpu_custom_call" | custom-call | tf_op jit(solution)/shard_map/attention_backward/pallas_call | solution.py:460
  53.6 2.0 %hand_over.1 = (bf16[256,512]{1,0:T(8,128)(2,1)}, bf16[256,512]{1,0:T(8,128)(2,1)}, bf16[256,512]{1,0:T(8,128)(2,1)}) custom-call(bf16[256,512]{1,0:T(8,128)(2,1)} %get-tuple-element.6.a, bf16[256,512]{1,0:T(8,128)(2,1)} %get-tuple-element.7.b, bf16[256,512]{1,0:T(8,128)(2,1)} %get-tuple-element.8.c), custom_call_target="tpu_custom_call" | custom-call | tf_op jit(solution)/shard_map/hand_over/pallas_call | solution.py:499

commit v6 on v5

--- a/solution.py
+++ b/solution.py
@@ -365,7 +365,15 @@
                 def _():
                     zc2[s].start()
 
-    key_side(1, probs_low, 8, 2)
+    for slot in (7, 6):
+        t = dot(
+            probs_low[pl.ds(slot * rows, rows), :],
+            qdf[1].reshape(total_q, HEAD_DIM),
+            NN,
+        )
+        xsend[1, slot] = t.astype(BF16)
+        xc[1, slot].start()
+    key_side(1, probs_low, 6, 2)
     query_side(4, 0)
     key_side(0, d_low, 8, 2)
     key_side(1, probs_low, 2, 0)

time: 55.8 us -> 55.8 us (level)
  no operation moved by 1% of the time
where the time goes in v6:
time: 55.8 us; the launch traced here: 55.6 us
  Pallas kernels  55 us (99%)
  between operations  0.64 us (1%)
    pallas_call x1, Pallas kernels, local(): pl.pallas_call(kernel, out_shape=[out, out, out], in_specs=[any_spec] * 4...  53 us
    pallas_call x1, Pallas kernels, local(): pl.pallas_call(hand_over, out_shape=[out, out, out], in_specs=[spec] * 3,...  2 us

profile of v6, /device:TPU:1, one launch (start us, length us, event | category | flops | bytes accessed | tf_op | source)
XLA Modules:
  0.0 55.6 jit_solution(9205777936518765084)
XLA Ops:
  0.6 53.0 %attention_backward.1 = (bf16[256,512]{1,0:T(8,128)(2,1)}, bf16[256,512]{1,0:T(8,128)(2,1)}, bf16[256,512]{1,0:T(8,128)(2,1)}) custom-call(bf16[256,128]{1,0:T(8,128)(2,1)} %q_in.1, bf16[256,128]{1,0:T(8,128)(2,1)} %k_in.1, bf16[256,128]{1,0:T(8,128)(2,1)} %v_in.1, bf16[256,128]{1,0:T(8,128)(2,1)} %do_in.1), custom_call_target="tpu_custom_call" | custom-call | tf_op jit(solution)/shard_map/attention_backward/pallas_call | solution.py:468
  53.6 2.0 %hand_over.1 = (bf16[256,512]{1,0:T(8,128)(2,1)}, bf16[256,512]{1,0:T(8,128)(2,1)}, bf16[256,512]{1,0:T(8,128)(2,1)}) custom-call(bf16[256,512]{1,0:T(8,128)(2,1)} %get-tuple-element.6.a, bf16[256,512]{1,0:T(8,128)(2,1)} %get-tuple-element.7.b, bf16[256,512]{1,0:T(8,128)(2,1)} %get-tuple-element.8.c), custom_call_target="tpu_custom_call" | custom-call | tf_op jit(solution)/shard_map/hand_over/pallas_call | solution.py:507
